TPU v7x, 32 devices: a whole 2x2x4 slice. The times are simulated.
32 devices in a mesh: rep: 16 (over z, x, core), shard: 2 (over y).
Axes of the slice: x: 2, y: 2, z: 4, core: 2. Of those that a mesh axis runs over, the one named last changes fastest.
Arguments:
- inputs: bfloat16 [32, 512, 576], P(('rep', 'shard')), may hold values from -6 to 6
- segments: int32 [32, 512], P(('rep', 'shard')), may hold values from 0 to 3, never falling along the last dimension, each value on 1 to 256 neighbouring positions
- cotangent: bfloat16 [32, 512, 576], P(('rep', 'shard')), may hold values from -6 to 6
- norm1_gain: bfloat16 [576], P('shard'), may hold values from 0.5 to 1.5
- w_query: bfloat16 [576, 576], P('shard'), may hold values from -0.25 to 0.25
- w_key: bfloat16 [576, 192], P('shard'), may hold values from -0.25 to 0.25
- w_value: bfloat16 [576, 192], P('shard'), may hold values from -0.25 to 0.25
- w_out: bfloat16 [576, 576], P('shard'), may hold values from -1.5 to 1.5
- norm2_gain: bfloat16 [576], P('shard'), may hold values from 0.5 to 1.5
- w_gate: bfloat16 [576, 1536], P('shard'), may hold values from -0.25 to 0.25
- w_up: bfloat16 [576, 1536], P('shard'), may hold values from -0.25 to 0.25
- w_down: bfloat16 [1536, 576], P('shard'), may hold values from -0.15625 to 0.15625
Outputs:
- output: bfloat16 [32, 512, 576], P(('rep', 'shard'))
- input_grad: bfloat16 [32, 512, 576], P(('rep', 'shard'))
- grad_norm1: float32 [576], P('shard')
- grad_query: float32 [576, 576], P('shard')
- grad_key: float32 [576, 192], P('shard')
- grad_value: float32 [576, 192], P('shard')
- grad_out: float32 [576, 576], P('shard')
- grad_norm2: float32 [576], P('shard')
- grad_gate: float32 [576, 1536], P('shard')
- grad_up: float32 [576, 1536], P('shard')
- grad_down: float32 [1536, 576], P('shard')
Inputs may be any that keep to these rules, and one draw needn't show every extreme that they name: `segments`: segment numbers never fall along a sequence; each segment has 1 to 256 tokens, one exactly that many.
All inputs are finite; a program needn't handle non-finite values.
Results may differ from a plain program's by a relative error of at most 0.02.
Values may be sent and summed in bfloat16 or wider, within the bound.
A program may use at most 128 MiB of HBM per device.

v0:
```python
import functools
import math

import jax
import jax.numpy as jnp
from jax import lax
from jax.experimental import pallas as pl
from jax.experimental.pallas import tpu as pltpu
from jax.sharding import PartitionSpec as P

HEAD_DIM = 64
MESH = pl.DeviceIdType.MESH
VMEM_LIMIT = 48 * 1024 * 1024


eps = 1e-05
rope_base = 100000.0


def rope_tables(seg_row, head_dim):
    count = seg_row.shape[0]
    index = jnp.arange(count, dtype=jnp.int32)
    before = jnp.concatenate([jnp.full((1,), -1, jnp.int32), seg_row[:-1]])
    starts = jnp.where(seg_row != before, index, jnp.zeros_like(index))
    place = (index - lax.cummax(starts, axis=0)).astype(jnp.float32)
    half = head_dim // 2
    freqs = jnp.exp(jnp.arange(half, dtype=jnp.float32) * (-2.0 * math.log(rope_base) / head_dim))
    angle = place[:, None] * freqs[None, :]
    return (jnp.cos(angle), jnp.sin(angle))


def rotate(values, cosine, sine, sign):
    half = values.shape[-1] // 2
    first = values[..., :half]
    second = values[..., half:]
    cos_b = cosine[:, None, :]
    sin_b = sine[:, None, :] * sign
    return jnp.concatenate(
        [first * cos_b - second * sin_b, second * cos_b + first * sin_b], axis=-1
    )


def attention_scores(queries, keys, allowed, scale):
    dots = jnp.einsum("tkgd,skd->kgts", queries, keys, preferred_element_type=jnp.float32) * scale
    return jnp.where(allowed[None, None], dots, -1e30)


def bits_of(size):
    return [1 << b for b in range(size.bit_length() - 1)]


def flipped(index, bit):
    return index + bit - 2 * bit * ((index // bit) % 2)


def greet(partners):
    barrier = pltpu.get_barrier_semaphore()
    for partner in partners:
        pl.semaphore_signal(barrier, inc=1, device_id=partner, device_id_type=MESH)
    pl.semaphore_wait(barrier, len(partners))


def gather_kernel(shards, share, dims, *refs):
    count = len(dims)
    blocks, outs = refs[:count], refs[count : 2 * count]
    send, recv, local = refs[2 * count :]
    r, s = lax.axis_index("rep"), lax.axis_index("shard")
    bits = list(reversed(bits_of(share)))
    others = [lax.rem(s + t, shards) for t in range(1, shards)]
    back = [lax.rem(s + shards - t, shards) for t in range(1, shards)]
    greet([(r, o) for o in others] + [(flipped(r, bit), s) for bit in bits])

    def part(ref, dim, owner):
        if dim is None:
            return (slice(None), slice(None))
        size = ref.shape[dim - (3 - len(ref.shape))] // share
        cut = pl.ds(pl.multiple_of(owner * size, size), size)
        return (cut, slice(None)) if dim == 1 else (slice(None), cut)

    held = {}
    copies, stays = [], []
    for a in range(count):
        own = pltpu.make_async_copy(blocks[a], outs[a].at[s], local.at[a])
        own.start()
        stays.append(own)
        held[a] = [lax.rem(r, share)]
        for t in range(1, shards):
            cut = part(blocks[a], dims[a], held[a][0])
            go = pltpu.make_async_remote_copy(
                src_ref=blocks[a].at[cut],
                dst_ref=outs[a].at[(s,) + cut],
                send_sem=send.at[a, t - 1, 0],
                recv_sem=recv.at[a, t - 1, 0],
                device_id=(r, others[t - 1]),
                device_id_type=MESH,
            )
            go.start()
            held[a, t] = [go]
    pending = {}
    for tick in range(count + len(bits)):
        for a in range(count):
            level = tick - a
            if dims[a] is None or not 0 <= level < len(bits):
                continue
            bit = bits[level]
            fresh = []
            for t in range(1, shards):
                arrived = held[a, t] if level == 0 else pending[a, t]
                for go in arrived:
                    go.wait_recv()
                now = []
                for j in range(1 << level):
                    owner = held[a][j]
                    cut = part(blocks[a], dims[a], owner)
                    where = outs[a].at[(back[t - 1],) + cut]
                    go = pltpu.make_async_remote_copy(
                        src_ref=where,
                        dst_ref=where,
                        send_sem=send.at[a, t - 1, (1 << level) + j],
                        recv_sem=recv.at[a, t - 1, (1 << level) + j],
                        device_id=(flipped(r, bit), s),
                        device_id_type=MESH,
                    )
                    go.start()
                    now.append(go)
                pending[a, t] = now
                copies.extend(arrived)
            held[a] = held[a] + [flipped(o, bit) for o in held[a]]
    for a in range(count):
        for t in range(1, shards):
            last = pending.get((a, t), held[a, t])
            for go in last:
                go.wait_recv()
            copies.extend(last)
    for go in copies:
        go.wait_send()
    for own in stays:
        own.wait()


def gather_weights(blocks, dims, shards, share):
    return pl.pallas_call(
        functools.partial(gather_kernel, shards, share, dims),
        out_shape=[jax.ShapeDtypeStruct((shards,) + b.shape, b.dtype) for b in blocks],
        in_specs=[pl.BlockSpec(memory_space=pltpu.VMEM)] * len(blocks),
        out_specs=[pl.BlockSpec(memory_space=pltpu.VMEM)] * len(blocks),
        scratch_shapes=[
            pltpu.SemaphoreType.DMA((len(blocks), max(1, shards - 1), share)),
            pltpu.SemaphoreType.DMA((len(blocks), max(1, shards - 1), share)),
            pltpu.SemaphoreType.DMA((len(blocks),)),
        ],
        compiler_params=pltpu.CompilerParams(
            collective_id=0, has_side_effects=True, vmem_limit_bytes=VMEM_LIMIT
        ),
    )(*blocks)


def plan_of(shape, shards, reps, splits):
    rep_bits, shard_bits = bits_of(reps), list(reversed(bits_of(shards)))
    size = list(shape)
    order = [("rep", rep_bits[0])] + [("shard", b) for b in shard_bits]
    order += [("rep", b) for b in rep_bits[1:]]
    steps = []
    for n, (axis, bit) in enumerate(order):
        dim = None
        if splits and axis == "shard":
            dim = 0
        elif splits and n < len(order) - 1:
            if size[1] % 32 == 0 and (size[2] % 256 != 0 or n == 0):
                dim = 1
            elif size[2] % 256 == 0:
                dim = 2
        if dim is not None:
            size[dim] //= 2
        steps.append((axis, bit, dim, tuple(size)))
    return steps


def reduce_kernel(plans, shards, count, *refs):
    grads, outs = refs[:count], refs[count : 2 * count]
    refs = refs[2 * count :]
    send, recv = refs[-2:]
    lands, at = [], 0
    for plan in plans:
        lands.append(refs[at : at + len(plan)])
        at += len(plan)
    r, s = lax.axis_index("rep"), lax.axis_index("shard")
    index = {"rep": r, "shard": s}

    def partner(axis, bit):
        return (flipped(r, bit), s) if axis == "rep" else (r, flipped(s, bit))

    greet([partner(axis, bit) for axis, bit, _, _ in plans[0]])

    def half(shape, dim, which):
        cut = [slice(None)] * 3
        size = shape[dim] // 2
        start = which * size
        cut[dim] = pl.ds(start if dim == 0 else pl.multiple_of(start, size), size)
        return tuple(cut)

    waits = []

    def start(c, n, src, dst, axis, bit):
        go = pltpu.make_async_remote_copy(
            src_ref=src,
            dst_ref=dst,
            send_sem=send.at[c, n],
            recv_sem=recv.at[c, n],
            device_id=partner(axis, bit),
            device_id_type=MESH,
        )
        go.start()
        waits.append(go)
        return go

    def stream(c):
        plan, cur = plans[c], grads[c]
        offset = [0, 0, 0]
        shape = cur.shape
        n = 0
        for step, (axis, bit, dim, after) in enumerate(plan):
            land = lands[c][step]
            on = (index[axis] // bit) % 2
            if dim is None:
                go = start(c, n, cur, land, axis, bit)
                yield
                go.wait_recv()
                land[...] = cur[...] + land[...]
            else:
                theirs = half(shape, dim, 1 - on)
                mine = half(shape, dim, on)
                go = start(c, n, cur.at[theirs], land, axis, bit)
                yield
                go.wait_recv()
                land[...] = cur[mine] + land[...]
                if axis == "rep":
                    offset[dim] = offset[dim] + on * after[dim]
            cur, shape = land, after
            n += 1
        out = outs[c]

        def place(offset, size):
            cut = []
            for d in (1, 2):
                if size[d] == out.shape[d]:
                    cut.append(slice(None))
                else:
                    unit = 16 if d == 1 else 128
                    cut.append(pl.ds(pl.multiple_of(offset[d], unit), size[d]))
            return (slice(None),) + tuple(cut)

        size = list(shape)
        out[place(offset, size)] = cur[...]
        for axis, bit, dim, after in reversed(plan):
            if axis == "shard" or dim is None:
                continue
            block = out.at[place(offset, size)]
            go = start(c, n, block, block, axis, bit)
            yield
            go.wait_recv()
            on = (index[axis] // bit) % 2
            offset[dim] = offset[dim] - on * after[dim]
            size[dim] *= 2
            n += 1

    streams = [stream(c) for c in range(count)]
    live = []
    while streams or live:
        if streams:
            live.append(streams.pop(0))
        for one in list(live):
            try:
                next(one)
            except StopIteration:
                live.remove(one)
    for go in waits:
        go.wait_send()


def reduce_grads(grads, splits, shards, reps):
    plans = [plan_of(g.shape, shards, reps, cut) for g, cut in zip(grads, splits)]
    outs, lands, most = [], [], 0
    for g, plan, cut in zip(grads, plans, splits):
        lead = 1 if cut else g.shape[0]
        outs.append(jax.ShapeDtypeStruct((lead,) + g.shape[1:], g.dtype))
        lands += [pltpu.VMEM(after, g.dtype) for _, _, _, after in plan]
        most = max(most, 2 * len(plan))
    return pl.pallas_call(
        functools.partial(reduce_kernel, plans, shards, len(grads)),
        out_shape=outs,
        in_specs=[pl.BlockSpec(memory_space=pltpu.VMEM)] * len(grads),
        out_specs=[pl.BlockSpec(memory_space=pltpu.VMEM)] * len(grads),
        scratch_shapes=lands
        + [
            pltpu.SemaphoreType.DMA((len(grads), most)),
            pltpu.SemaphoreType.DMA((len(grads), most)),
        ],
        compiler_params=pltpu.CompilerParams(
            collective_id=1, has_side_effects=True, vmem_limit_bytes=VMEM_LIMIT
        ),
    )(*grads)


def body(
    shards,
    reps,
    inputs,
    segments,
    cotangent,
    norm1_gain,
    w_query,
    w_key,
    w_value,
    w_out,
    norm2_gain,
    w_gate,
    w_up,
    w_down,
):
    share = 4 if reps % 4 == 0 else 1
    w_attn = jnp.concatenate([w_query, w_key, w_value, w_out], axis=1)
    w_gain = jnp.zeros((16, norm1_gain.shape[0]), norm1_gain.dtype)
    w_gain = w_gain.at[0].set(norm1_gain).at[1].set(norm2_gain)
    nq, nk = w_query.shape[1], w_key.shape[1]
    w_all = gather_weights(
        [w_attn, w_gate, w_up, w_down, w_gain], [2, 2, 2, 1, None], shards, share
    )
    wa, wg, wu, wd = [w.reshape(-1, w.shape[2]) for w in w_all[:4]]
    gain_one, gain_two = w_all[4][:, 0].reshape(-1), w_all[4][:, 1].reshape(-1)
    wq, wk, wv = wa[:, :nq], wa[:, nq : nq + nk], wa[:, nq + nk : nq + 2 * nk]
    wo = wa[:, nq + 2 * nk :]
    x = inputs[0].astype(jnp.float32)
    seg_row = segments[0]
    count = x.shape[0]
    width = x.shape[1]
    kv_heads = wk.shape[1] // HEAD_DIM
    heads = wq.shape[1] // HEAD_DIM
    group = heads // kv_heads
    scale = HEAD_DIM ** (-0.5)
    cosine, sine = rope_tables(seg_row, HEAD_DIM)
    index = jnp.arange(count)
    allowed = (seg_row[:, None] == seg_row[None, :]) & (index[:, None] >= index[None, :])
    g_one = gain_one.astype(jnp.float32)
    r_one = lax.rsqrt(jnp.mean(x * x, axis=1, keepdims=True) + eps)
    h_one = (x * r_one * g_one).astype(jnp.bfloat16)
    q_lin = jnp.dot(h_one, wq, preferred_element_type=jnp.float32)
    k_lin = jnp.dot(h_one, wk, preferred_element_type=jnp.float32)
    values = (
        jnp.dot(h_one, wv, preferred_element_type=jnp.float32)
        .astype(jnp.bfloat16)
        .reshape(count, kv_heads, HEAD_DIM)
    )
    queries = (
        rotate(q_lin.reshape(count, heads, HEAD_DIM), cosine, sine, 1.0)
        .astype(jnp.bfloat16)
        .reshape(count, kv_heads, group, HEAD_DIM)
    )
    keys = rotate(k_lin.reshape(count, kv_heads, HEAD_DIM), cosine, sine, 1.0).astype(jnp.bfloat16)
    scores = attention_scores(queries, keys, allowed, scale)
    top = jnp.max(scores, axis=3, keepdims=True)
    expo = jnp.exp(scores - top)
    total = jnp.sum(expo, axis=3, keepdims=True)
    lse = top + jnp.log(total)
    probs = (expo / total).astype(jnp.bfloat16)
    mixed = jnp.einsum("kgts,skd->tkgd", probs, values, preferred_element_type=jnp.float32)
    mixed_b = mixed.reshape(count, width).astype(jnp.bfloat16)
    y_one = x + jnp.dot(mixed_b, wo, preferred_element_type=jnp.float32)
    g_two = gain_two.astype(jnp.float32)
    r_two = lax.rsqrt(jnp.mean(y_one * y_one, axis=1, keepdims=True) + eps)
    h_two = (y_one * r_two * g_two).astype(jnp.bfloat16)
    gate = jnp.dot(h_two, wg, preferred_element_type=jnp.float32)
    up_val = jnp.dot(h_two, wu, preferred_element_type=jnp.float32)
    sigm = jax.nn.sigmoid(gate)
    hidden = (gate * sigm * up_val).astype(jnp.bfloat16)
    output = y_one + jnp.dot(hidden, wd, preferred_element_type=jnp.float32)
    bq, bk, bv, bo, bg, bu, bd = wq, wk, wv, wo, wg, wu, wd
    d_out = cotangent[0].astype(jnp.float32)
    d_out_b = d_out.astype(jnp.bfloat16)
    grad_down = jnp.einsum("tf,td->fd", hidden, d_out_b, preferred_element_type=jnp.float32)
    d_hidden = jnp.einsum("td,fd->tf", d_out_b, bd, preferred_element_type=jnp.float32)
    d_up = (d_hidden * gate * sigm).astype(jnp.bfloat16)
    d_gate = (d_hidden * up_val * sigm * (1.0 + gate * (1.0 - sigm))).astype(jnp.bfloat16)
    grad_gate = jnp.einsum("td,tf->df", h_two, d_gate, preferred_element_type=jnp.float32)
    grad_up = jnp.einsum("td,tf->df", h_two, d_up, preferred_element_type=jnp.float32)
    d_h_two = jnp.einsum("tf,df->td", d_gate, bg, preferred_element_type=jnp.float32) + jnp.einsum(
        "tf,df->td", d_up, bu, preferred_element_type=jnp.float32
    )
    grad_gain_two = jnp.sum(d_h_two * y_one * r_two, axis=0)
    u_two = d_h_two * g_two
    d_y_one = (
        d_out + r_two * u_two - y_one * r_two**3 * jnp.mean(u_two * y_one, axis=1, keepdims=True)
    )
    d_attn = d_y_one.astype(jnp.bfloat16)
    grad_wo = jnp.einsum("td,te->de", mixed_b, d_attn, preferred_element_type=jnp.float32)
    d_mixed = (
        jnp.einsum("te,de->td", d_attn, bo, preferred_element_type=jnp.float32)
        .astype(jnp.bfloat16)
        .reshape(count, kv_heads, group, HEAD_DIM)
    )
    probs_f = jnp.exp(attention_scores(queries, keys, allowed, scale) - lse)
    probs_b = probs_f.astype(jnp.bfloat16)
    d_probs = jnp.einsum("tkgd,skd->kgts", d_mixed, values, preferred_element_type=jnp.float32)
    delta = jnp.sum(d_probs * probs_f, axis=3, keepdims=True)
    d_scores = (probs_f * (d_probs - delta)).astype(jnp.bfloat16)
    d_queries = (
        jnp.einsum("kgts,skd->tkgd", d_scores, keys, preferred_element_type=jnp.float32) * scale
    )
    d_keys = (
        jnp.einsum("kgts,tkgd->skd", d_scores, queries, preferred_element_type=jnp.float32) * scale
    )
    d_values = jnp.einsum("kgts,tkgd->skd", probs_b, d_mixed, preferred_element_type=jnp.float32)
    dq_b = (
        rotate(d_queries.reshape(count, heads, HEAD_DIM), cosine, sine, -1.0)
        .reshape(count, width)
        .astype(jnp.bfloat16)
    )
    dk_b = (
        rotate(d_keys, cosine, sine, -1.0).reshape(count, kv_heads * HEAD_DIM).astype(jnp.bfloat16)
    )
    dv_b = d_values.reshape(count, kv_heads * HEAD_DIM).astype(jnp.bfloat16)
    grad_wq = jnp.einsum("td,te->de", h_one, dq_b, preferred_element_type=jnp.float32)
    grad_wk = jnp.einsum("td,te->de", h_one, dk_b, preferred_element_type=jnp.float32)
    grad_wv = jnp.einsum("td,te->de", h_one, dv_b, preferred_element_type=jnp.float32)
    d_h_one = jnp.einsum("te,de->td", dq_b, bq, preferred_element_type=jnp.float32)
    d_h_one = d_h_one + jnp.einsum("te,de->td", dk_b, bk, preferred_element_type=jnp.float32)
    d_h_one = d_h_one + jnp.einsum("te,de->td", dv_b, bv, preferred_element_type=jnp.float32)
    grad_gain_one = jnp.sum(d_h_one * x * r_one, axis=0)
    u_one = d_h_one * g_one
    d_x = d_y_one + r_one * u_one - x * r_one**3 * jnp.mean(u_one * x, axis=1, keepdims=True)
    low = jnp.bfloat16
    g_attn = jnp.concatenate([grad_wq, grad_wk, grad_wv, grad_wo], axis=1)
    g_gains = jnp.zeros((1, 8, width), jnp.float32)
    g_gains = g_gains.at[0, 0].set(grad_gain_one).at[0, 1].set(grad_gain_two)
    parts = [
        g.astype(low).reshape(shards, -1, g.shape[1])
        for g in (grad_down, grad_gate, grad_up, g_attn)
    ]
    sums = reduce_grads(parts + [g_gains], [True] * 4 + [False], shards, reps)
    t_down, t_gate, t_up, t_attn = [t[0].astype(jnp.float32) for t in sums[:4]]
    g_gains = sums[4][0, :2]
    own = width // shards
    g_gains = lax.dynamic_slice_in_dim(g_gains, lax.axis_index("shard") * own, own, 1)
    return (
        output.astype(low)[None],
        d_x.astype(low)[None],
        g_gains[0],
        t_attn[:, :nq],
        t_attn[:, nq : nq + nk],
        t_attn[:, nq + nk : nq + 2 * nk],
        t_attn[:, nq + 2 * nk :],
        g_gains[1],
        t_gate,
        t_up,
        t_down,
    )


def solution(mesh):
    return jax.shard_map(
        functools.partial(body, mesh.shape["shard"], mesh.shape["rep"]),
        mesh=mesh,
        in_specs=(
            P(("rep", "shard"), None, None),
            P(("rep", "shard"), None),
            P(("rep", "shard"), None, None),
            P("shard"),
            P("shard", None),
            P("shard", None),
            P("shard", None),
            P("shard", None),
            P("shard"),
            P("shard", None),
            P("shard", None),
            P("shard", None),
        ),
        out_specs=(
            P(("rep", "shard"), None, None),
            P(("rep", "shard"), None, None),
            P("shard"),
            P("shard", None),
            P("shard", None),
            P("shard", None),
            P("shard", None),
            P("shard"),
            P("shard", None),
            P("shard", None),
            P("shard", None),
        ),
        check_vma=False,
    )
```

profile of v0, /device:TPU:0, one launch (start us, length us, event | category | flops | bytes accessed | tf_op | source)
XLA Modules:
  0.0 232.4 jit_solution(8721102309359863158)
XLA Ops:
  0.7 2.4 %concatenate.41.refs_0_ = bf16[288,1536]{1,0:T(8,128)(2,1)} concatenate(bf16[288,576]{1,0:T(8,128)(2,1)} %param.24, bf16[288,192]{1,0:T(8,128)(2,1)} %param.25, bf16[288,192]{1,0:T(8,128)(2,1)} %param.26, bf16[288,576]{1,0:T(8,128)(2,1)} %param.27), dimensions={1} | concatenate | bytes 1769472 | tf_op jit(solution)/shard_map/concatenate | solution.py:322
  7.3 35.9 %shard_map.203 = (bf16[2,288,1536]{2,1,0:T(8,128)(2,1)S(1)}, bf16[2,288,1536]{2,1,0:T(8,128)(2,1)}, bf16[2,288,1536]{2,1,0:T(8,128)(2,1)}, bf16[2,768,576]{2,1,0:T(8,128)(2,1)}, bf16[2,16,288]{2,1,0:T(8,128)(2,1)S(1)}) custom-call(bf16[288,1536]{1,0:T(8,128)(2,1)S(1)} %copy-done, bf16[288,1536]{1,0:T(8,128)(2,1)S(1)} %copy-done.1, ...), custom_call_target="tpu_custom_call" | custom-call | tf_op jit(solution)/shard_map/pallas_call | solution.py:142
  46.7 3.0 %fusion.47 = f32[512,9,64]{0,2,1:T(8,128)} fusion(bf16[9,64,576]{2,1,0:T(8,128)(2,1)} %bitcast.231, bf16[1,512,576]{1,2,0:T(8,128)(2,1)S(1)} %fusion.33), kind=kOutput, calls=%fused_computation.82 | convolution fusion | flops 339738624 | bytes 2433024 | tf_op jit(solution)/shard_map/dot_general | solution.py:347
  51.3 2.3 subtract_convert_fusion
  56.2 2.7 %fusion.65 = (f32[3,3,512]{2,1,0:T(4,128)S(1)}, f32[3,3,512,512]{2,3,1,0:T(8,128)S(1)}) fusion(bf16[512,3,3,32]{0,3,2,1:T(8,128)(2,1)} %bitcast.228, bf16[512,3,3,32]{0,3,2,1:T(8,128)(2,1)} %bitcast.226, bf16[512,3,32]{0,2,1:T(8,128)(2,1)S(1)} %get-tuple-element.123, bf16[512,3,32]{0,2,1:T(8,128)(2,1)S(1)} %get-tuple-element.122, ...), kind=kOutput, calls=%fused_computation.130 | convolution fusion | flops 310636032 | bytes 10504192 | tf_op jit(solution)/shard_map/tkgd,skd->kgts/dot_general | solution.py:44
  60.3 2.3 copy-done.8
  62.6 1.7 fusion.16
  64.4 1.7 multiply_reduce_fusion.2
  71.2 2.9 %multiply_convert_fusion = (bf16[512,1536]{1,0:T(8,128)(2,1)S(1)}, bf16[512,1536]{1,0:T(8,128)(2,1)S(1)}, bf16[512,1536]{1,0:T(8,128)(2,1)S(1)}) fusion(f32[512,1536]{1,0:T(8,128)S(1)} %fusion.66, f32[512,1536]{1,0:T(8,128)S(1)} %fusion.67, bf16[1536,576]{1,0:T(8,128)(2,1)S(1)} %bitcast.239, bf16[1,512,576]{1,2,0:T(8,128)(2,1)S(1)} %copy-done.31), kind=kOutput, calls=%fused_computation.15 | convolution fusion | flops 918552576 | bytes 13369344 | tf_op jit(solution)/shard_map/td,fd->tf/dot_general | solution.py:381
  74.1 1.9 fusion.17
  78.6 1.7 multiply_subtract_fusion
  81.5 5.3 %fusion = (f32[3,3,512]{2,1,0:T(4,128)}, f32[3,512,512,3]{2,1,3,0:T(8,128)}) fusion(f32[3,3,512,512]{2,3,1,0:T(8,128)S(1)} %bitcast.209, f32[3,3,512]{2,1,0:T(4,128)S(1)} %log_add_fusion, bf16[512,3,64,1]{0,2,3,1:T(8,128)(2,1)S(1)} %bitcast.235, bf16[512,3,3,64]{0,3,2,1:T(8,128)(2,1)S(1)} %bitcast.216), kind=kOutput, calls=%fused_computation.2 | convolution fusion | flops 309063168 | bytes 19697664 | tf_op jit(solution)/shard_map/tkgd,skd->kgts/dot_general | solution.py:403
  86.8 11.1 %fusion.2 = bf16[3,3,512,512]{2,3,1,0:T(8,128)(2,1)} fusion(f32[3,512,512,3]{2,1,3,0:T(8,128)} %get-tuple-element.137, f32[3,3,512,512]{2,3,1,0:T(8,128)} %copy-done.8, f32[3,3,512]{2,1,0:T(4,128)} %get-tuple-element.136, f32[3,3,512]{2,1,0:T(4,128)} %copy-done.40), kind=kLoop, calls=%fused_computation.4 | loop fusion | flops 9437184 | bytes 23629824 | tf_op jit(solution)/shard_map/convert_element_type | solution.py:405
  98.0 3.5 %convolution_multiply_fusion = f32[3,64,3,512]{3,1,2,0:T(8,128)S(1)} fusion(bf16[3,3,512,512]{2,3,1,0:T(8,128)(2,1)} %fusion.2, bf16[512,3,32]{0,2,1:T(8,128)(2,1)} %copy-done.39, bf16[512,3,32]{0,2,1:T(8,128)(2,1)} %copy-done.38), kind=kOutput, calls=%fused_computation.32 | convolution fusion | flops 302678016 | bytes 6094848 | tf_op jit(solution)/shard_map/kgts,skd->tkgd/dot_general | solution.py:407
  101.5 1.8 multiply_subtract_fusion.1
  104.9 1.5 fusion.22
  107.7 1.6 fusion.34
  112.8 2.3 copy.41
  115.1 2.8 %convolution_convert_fusion.2 = bf16[576,1536]{1,0:T(8,128)(2,1)S(1)} fusion(bf16[512,576]{0,1:T(8,128)(2,1)} %copy-done.35, bf16[512,1536]{1,0:T(8,128)(2,1)} %copy-done.59), kind=kOutput, calls=%fused_computation.21 | convolution fusion | flops 906854400 | bytes 3932160 | tf_op jit(solution)/shard_map/td,tf->df/dot_general | solution.py:384
  118.0 2.3 convolution_convert_fusion.1
  125.4 4.0 %concatenate.50.refs_3_ = bf16[2,288,1536]{2,1,0:T(8,128)(2,1)} concatenate(bf16[2,288,576]{2,1,0:T(8,128)(2,1)} %convolution_convert_fusion.4, bf16[2,288,192]{2,1,0:T(8,128)(2,1)S(1)} %copy-done.28, bf16[2,288,192]{2,1,0:T(8,128)(2,1)S(1)} %copy-done.29, bf16[2,288,576]{2,1,0:T(8,128)(2,1)} %convolution_convert_fusion.3), dimensions={2} | concatenate | bytes 3538944 | tf_op jit(solution)/shard_map/concatenate | solution.py:432
  131.0 87.9 %shard_map.204 = (bf16[1,768,576]{2,1,0:T(8,128)(2,1)S(1)}, bf16[1,288,1536]{2,1,0:T(8,128)(2,1)S(1)}, bf16[1,288,1536]{2,1,0:T(8,128)(2,1)S(1)}, bf16[1,288,1536]{2,1,0:T(8,128)(2,1)S(1)}, f32[1,8,576]{2,1,0:T(8,128)S(1)}) custom-call(bf16[2,768,576]{2,1,0:T(8,128)(2,1)} %bitcast.215, bf16[2,288,1536]{2,1,0:T(8,128)(2,1)S(1)} %bitcast.207, ...), custom_call_target="tpu_custom_call" | custom-call | tf_op jit(solution)/shard_map/pallas_call | solution.py:289
  226.0 2.3 bitcast_convert_fusion.1
  229.6 2.8 %copy.42 = f32[768,576]{0,1:T(8,128)} copy(f32[768,576]{1,0:T(8,128)} %bitcast_convert_fusion) | data formatting | bytes 3538944
  (195 shorter events, 43.3 us)
Async XLA Ops:
  0.7 3.0 %copy-start.50 = (bf16[288]{0:T(512)(128)(2,1)S(1)}, bf16[288]{0:T(512)(128)(2,1)}, u32[]{:S(2)}) copy-start(bf16[288]{0:T(512)(128)(2,1)} %param.23) | copy-start | bytes 1732
  0.7 3.1 %copy-start.51 = (bf16[288]{0:T(512)(128)(2,1)S(1)}, bf16[288]{0:T(512)(128)(2,1)}, u32[]{:S(2)}) copy-start(bf16[288]{0:T(512)(128)(2,1)} %param.28) | copy-start | bytes 1732
  7.3 36.1 %copy-start.14 = (bf16[1,512,576]{1,2,0:T(8,128)(2,1)S(1)}, bf16[1,512,576]{1,2,0:T(8,128)(2,1)}, u32[]{:S(2)}) copy-start(bf16[1,512,576]{1,2,0:T(8,128)(2,1)} %param.20) | copy-start | bytes 1769476
  46.7 7.9 %copy-start.12 = (bf16[1,512,576]{1,2,0:T(8,128)(2,1)}, bf16[1,512,576]{1,2,0:T(8,128)(2,1)S(1)}, u32[]{:S(2)}) copy-start(bf16[1,512,576]{1,2,0:T(8,128)(2,1)S(1)} %fusion.33) | copy-start | bytes 1769476
  46.7 3.0 %copy-start.48 = (s32[1,512]{1,0:T(1,128)S(1)}, s32[1,512]{1,0:T(1,128)}, u32[]{:S(2)}) copy-start(s32[1,512]{1,0:T(1,128)} %param.21) | copy-start | bytes 6148
  51.3 4.5 %copy-start.24 = (f32[512,32]{0,1:T(8,128)}, f32[512,32]{0,1:T(8,128)S(1)}, u32[]{:S(2)}) copy-start(f32[512,32]{0,1:T(8,128)S(1)} %get-tuple-element.126) | copy-start | bytes 196612
  55.9 2.9 %copy-start.38 = (bf16[512,3,32]{0,2,1:T(8,128)(2,1)}, bf16[512,3,32]{0,2,1:T(8,128)(2,1)S(1)}, u32[]{:S(2)}) copy-start(bf16[512,3,32]{0,2,1:T(8,128)(2,1)S(1)} %get-tuple-element.122) | copy-start | bytes 294916
  56.0 2.9 %copy-start.39 = (bf16[512,3,32]{0,2,1:T(8,128)(2,1)}, bf16[512,3,32]{0,2,1:T(8,128)(2,1)S(1)}, u32[]{:S(2)}) copy-start(bf16[512,3,32]{0,2,1:T(8,128)(2,1)S(1)} %get-tuple-element.123) | copy-start | bytes 294916
  58.9 3.7 %copy-start.8 = (f32[3,3,512,512]{2,3,1,0:T(8,128)}, f32[3,3,512,512]{2,3,1,0:T(8,128)S(1)}, u32[]{:S(2)}) copy-start(f32[3,3,512,512]{2,3,1,0:T(8,128)S(1)} %get-tuple-element.132) | copy-start | bytes 28311556
  58.9 3.7 %copy-start.44 = (f32[3,3,512]{2,1,0:T(4,128)}, f32[3,3,512]{2,1,0:T(4,128)S(1)}, u32[]{:S(2)}) copy-start(f32[3,3,512]{2,1,0:T(4,128)S(1)} %get-tuple-element.131) | copy-start | bytes 55300
  58.9 3.7 %copy-start.42 = (bf16[512,192]{0,1:T(8,128)(2,1)S(1)}, bf16[512,192]{0,1:T(8,128)(2,1)}, u32[]{:S(2)}) copy-start(bf16[512,192]{0,1:T(8,128)(2,1)} %convolution_convert_fusion.8) | copy-start | bytes 589828
  66.0 11.1 %copy-start.17 = (f32[512,576]{0,1:T(8,128)}, f32[512,576]{0,1:T(8,128)S(1)}, u32[]{:S(2)}) copy-start(f32[512,576]{0,1:T(8,128)S(1)} %get-tuple-element.134) | copy-start | bytes 3538948
  74.1 3.1 %copy-start.55 = (bf16[512,1536]{1,0:T(8,128)(2,1)}, bf16[512,1536]{1,0:T(8,128)(2,1)S(1)}, u32[]{:S(2)}) copy-start(bf16[512,1536]{1,0:T(8,128)(2,1)S(1)} %get-tuple-element.109) | copy-start | bytes 4718596
  74.1 7.0 %slice-start = ((s8[9437184]{0:T(1024)(128)(4,1)}), s8[4194304]{0:T(1024)(128)(4,1)S(1)}, s32[]{:S(2)}) async-start(s8[9437184]{0:T(1024)(128)(4,1)} %bitcast.208), calls=%async_computation | async-start | bytes 8388608
  76.0 5.1 %slice-start.1 = ((s8[9437184]{0:T(1024)(128)(4,1)}), s8[4194304]{0:T(1024)(128)(4,1)S(1)}, s32[]{:S(2)}) async-start(s8[9437184]{0:T(1024)(128)(4,1)} %bitcast.208), calls=%async_computation.1 | async-start | bytes 8388608
  77.2 4.0 %slice-start.2 = ((s8[9437184]{0:T(1024)(128)(4,1)}), s8[1048576]{0:T(1024)(128)(4,1)S(1)}, s32[]{:S(2)}) async-start(s8[9437184]{0:T(1024)(128)(4,1)} %bitcast.208), calls=%async_computation.2 | async-start | bytes 2097152
  80.4 29.6 %copy-start.10 = (f32[512,576]{0,1:T(8,128)}, f32[512,576]{0,1:T(8,128)S(1)}, u32[]{:S(2)}) copy-start(f32[512,576]{0,1:T(8,128)S(1)} %multiply_subtract_fusion) | copy-start | bytes 3538948
  80.4 6.4 %copy-start.40 = (f32[3,3,512]{2,1,0:T(4,128)}, f32[3,3,512]{2,1,0:T(4,128)S(1)}, u32[]{:S(2)}) copy-start(f32[3,3,512]{2,1,0:T(4,128)S(1)} %log_add_fusion) | copy-start | bytes 55300
  81.1 5.7 %copy-start.15 = (bf16[512,576]{0,1:T(8,128)(2,1)}, bf16[512,576]{0,1:T(8,128)(2,1)S(1)}, u32[]{:S(2)}) copy-start(bf16[512,576]{0,1:T(8,128)(2,1)S(1)} %convolution_convert_fusion.5) | copy-start | bytes 1769476
  98.0 6.9 %copy-start.9 = (bf16[3,3,512,512]{2,3,1,0:T(8,128)(2,1)S(1)}, bf16[3,3,512,512]{2,3,1,0:T(8,128)(2,1)}, u32[]{:S(2)}) copy-start(bf16[3,3,512,512]{2,3,1,0:T(8,128)(2,1)} %fusion.2) | copy-start | bytes 14155780
  98.0 6.9 %copy-start.26 = (bf16[512,9,32]{0,2,1:T(8,128)(2,1)S(1)}, bf16[512,9,32]{0,2,1:T(8,128)(2,1)}, u32[]{:S(2)}) copy-start(bf16[512,9,32]{0,2,1:T(8,128)(2,1)} %get-tuple-element.118) | copy-start | bytes 884740
  98.0 6.9 %copy-start.27 = (bf16[512,9,32]{0,2,1:T(8,128)(2,1)S(1)}, bf16[512,9,32]{0,2,1:T(8,128)(2,1)}, u32[]{:S(2)}) copy-start(bf16[512,9,32]{0,2,1:T(8,128)(2,1)} %get-tuple-element.119) | copy-start | bytes 884740
  98.0 9.7 %slice-start.3 = ((s8[9437184]{0:T(1024)(128)(4,1)}), s8[4194304]{0:T(1024)(128)(4,1)S(1)}, s32[]{:S(2)}) async-start(s8[9437184]{0:T(1024)(128)(4,1)} %bitcast.210), calls=%async_computation.3 | async-start | bytes 8388608
  101.5 6.2 %slice-start.4 = ((s8[9437184]{0:T(1024)(128)(4,1)}), s8[4194304]{0:T(1024)(128)(4,1)S(1)}, s32[]{:S(2)}) async-start(s8[9437184]{0:T(1024)(128)(4,1)} %bitcast.210), calls=%async_computation.4 | async-start | bytes 8388608
  (42 other events, 69.8 us)
where the time goes:
time: 233 us; the launch traced here: 232 us
  Pallas kernels  124 us (53%)
  matrix products  47.1 us (20%)
  local copies, waits for them, and re-layouts  31.7 us (14%)
  other arithmetic  28.3 us (12%)
    pallas_call x1, Pallas kernels, reduce_grads(): pl.pallas_call(functools.partial(reduce_kernel, plans, shards, len(grads)...  87.9 us
    pallas_call x1, Pallas kernels, gather_weights(): pl.pallas_call(functools.partial(gather_kernel, shards, share, dims), out...  35.9 us
    unnamed x134, local copies, waits for them, and re-layouts  15.9 us
    convert_element_type x1, other arithmetic, body(): d_scores = (probs_f * (d_probs - delta)).astype(jnp.bfloat16)  11.1 us
    dot_general x1, matrix products, body(): jnp.einsum('tkgd,skd->kgts', d_mixed, values, preferred_element_type=jnp....  5.32 us
    convert_element_type x3, other arithmetic, body(): t_down, t_gate, t_up, t_attn = [t[0].astype(jnp.float32) for t in sums[:4]]  5.06 us

commit v1 on v0

--- a/solution.py
+++ b/solution.py
@@ -155,11 +155,12 @@
     )(*blocks)
 
 
-def plan_of(shape, shards, reps, splits):
+def plan_of(shape, shards, reps, splits, turn):
     rep_bits, shard_bits = bits_of(reps), list(reversed(bits_of(shards)))
     size = list(shape)
-    order = [("rep", rep_bits[0])] + [("shard", b) for b in shard_bits]
-    order += [("rep", b) for b in rep_bits[1:]]
+    order = [("rep", b) for b in rep_bits]
+    first = 2 if turn % 2 else 1
+    order[first:first] = [("shard", b) for b in shard_bits]
     steps = []
     for n, (axis, bit) in enumerate(order):
         dim = None
@@ -199,7 +200,7 @@
         cut[dim] = pl.ds(start if dim == 0 else pl.multiple_of(start, size), size)
         return tuple(cut)
 
-    waits = []
+    waits, free, clock = [], {}, [0.0]
 
     def start(c, n, src, dst, axis, bit):
         go = pltpu.make_async_remote_copy(
@@ -212,7 +213,11 @@
         )
         go.start()
         waits.append(go)
-        return go
+        link = (axis, bit)
+        rate = 300e3 if link == ("rep", 1) else 50e3
+        begin = max(clock[0], free.get(link, 0.0))
+        free[link] = begin + math.prod(src.shape) * 2 / rate
+        return go, free[link] + 1.5
 
     def stream(c):
         plan, cur = plans[c], grads[c]
@@ -223,15 +228,15 @@
             land = lands[c][step]
             on = (index[axis] // bit) % 2
             if dim is None:
-                go = start(c, n, cur, land, axis, bit)
-                yield
+                go, due = start(c, n, cur, land, axis, bit)
+                yield due
                 go.wait_recv()
                 land[...] = cur[...] + land[...]
             else:
                 theirs = half(shape, dim, 1 - on)
                 mine = half(shape, dim, on)
-                go = start(c, n, cur.at[theirs], land, axis, bit)
-                yield
+                go, due = start(c, n, cur.at[theirs], land, axis, bit)
+                yield due
                 go.wait_recv()
                 land[...] = cur[mine] + land[...]
                 if axis == "rep":
@@ -256,8 +261,8 @@
             if axis == "shard" or dim is None:
                 continue
             block = out.at[place(offset, size)]
-            go = start(c, n, block, block, axis, bit)
-            yield
+            go, due = start(c, n, block, block, axis, bit)
+            yield due
             go.wait_recv()
             on = (index[axis] // bit) % 2
             offset[dim] = offset[dim] - on * after[dim]
@@ -265,21 +270,19 @@
             n += 1
 
     streams = [stream(c) for c in range(count)]
-    live = []
-    while streams or live:
-        if streams:
-            live.append(streams.pop(0))
-        for one in list(live):
-            try:
-                next(one)
-            except StopIteration:
-                live.remove(one)
+    due = [(next(one), c) for c, one in enumerate(streams)]
+    while due:
+        due.sort()
+        clock[0], c = due.pop(0)
+        then = next(streams[c], None)
+        if then is not None:
+            due.append((then, c))
     for go in waits:
         go.wait_send()
 
 
 def reduce_grads(grads, splits, shards, reps):
-    plans = [plan_of(g.shape, shards, reps, cut) for g, cut in zip(grads, splits)]
+    plans = [plan_of(g.shape, shards, reps, cut, i) for i, (g, cut) in enumerate(zip(grads, splits))]
     outs, lands, most = [], [], 0
     for g, plan, cut in zip(grads, plans, splits):
         lead = 1 if cut else g.shape[0]

time: 233 us -> 231 us (level)
  Pallas kernels: 124 us -> 121 us
    pallas_call x1, Pallas kernels: 87.9 us -> 85.2 us  [reduce_grads(): pl.pallas_call(functools.partial(reduce_kernel, plans, shards, len(grads)...]
where the time goes in v1:
time: 231 us; the launch traced here: 230 us
  Pallas kernels  121 us (52%)
  matrix products  47.1 us (20%)
  local copies, waits for them, and re-layouts  31.7 us (14%)
  other arithmetic  28.3 us (12%)
    pallas_call x1, Pallas kernels, reduce_grads(): pl.pallas_call(functools.partial(reduce_kernel, plans, shards, len(grads)...  85.2 us
    pallas_call x1, Pallas kernels, gather_weights(): pl.pallas_call(functools.partial(gather_kernel, shards, share, dims), out...  35.9 us
    unnamed x134, local copies, waits for them, and re-layouts  15.9 us
    convert_element_type x1, other arithmetic, body(): d_scores = (probs_f * (d_probs - delta)).astype(jnp.bfloat16)  11.1 us
    dot_general x1, matrix products, body(): jnp.einsum('tkgd,skd->kgts', d_mixed, values, preferred_element_type=jnp....  5.32 us
    convert_element_type x3, other arithmetic, body(): t_down, t_gate, t_up, t_attn = [t[0].astype(jnp.float32) for t in sums[:4]]  5.06 us

profile of v1, /device:TPU:0, one launch (start us, length us, event | category | flops | bytes accessed | tf_op | source)
XLA Modules:
  0.0 229.7 jit_solution(18115451523915292260)
XLA Ops:
  0.7 2.4 %concatenate.41.refs_0_ = bf16[288,1536]{1,0:T(8,128)(2,1)} concatenate(bf16[288,576]{1,0:T(8,128)(2,1)} %param.24, bf16[288,192]{1,0:T(8,128)(2,1)} %param.25, bf16[288,192]{1,0:T(8,128)(2,1)} %param.26, bf16[288,576]{1,0:T(8,128)(2,1)} %param.27), dimensions={1} | concatenate | bytes 1769472 | tf_op jit(solution)/shard_map/concatenate | solution.py:325
  7.3 35.9 %shard_map.203 = (bf16[2,288,1536]{2,1,0:T(8,128)(2,1)S(1)}, bf16[2,288,1536]{2,1,0:T(8,128)(2,1)}, bf16[2,288,1536]{2,1,0:T(8,128)(2,1)}, bf16[2,768,576]{2,1,0:T(8,128)(2,1)}, bf16[2,16,288]{2,1,0:T(8,128)(2,1)S(1)}) custom-call(bf16[288,1536]{1,0:T(8,128)(2,1)S(1)} %copy-done, bf16[288,1536]{1,0:T(8,128)(2,1)S(1)} %copy-done.1, ...), custom_call_target="tpu_custom_call" | custom-call | tf_op jit(solution)/shard_map/pallas_call | solution.py:142
  46.7 3.0 %fusion.47 = f32[512,9,64]{0,2,1:T(8,128)} fusion(bf16[9,64,576]{2,1,0:T(8,128)(2,1)} %bitcast.231, bf16[1,512,576]{1,2,0:T(8,128)(2,1)S(1)} %fusion.33), kind=kOutput, calls=%fused_computation.82 | convolution fusion | flops 339738624 | bytes 2433024 | tf_op jit(solution)/shard_map/dot_general | solution.py:350
  51.3 2.3 subtract_convert_fusion
  56.2 2.7 %fusion.65 = (f32[3,3,512]{2,1,0:T(4,128)S(1)}, f32[3,3,512,512]{2,3,1,0:T(8,128)S(1)}) fusion(bf16[512,3,3,32]{0,3,2,1:T(8,128)(2,1)} %bitcast.228, bf16[512,3,3,32]{0,3,2,1:T(8,128)(2,1)} %bitcast.226, bf16[512,3,32]{0,2,1:T(8,128)(2,1)S(1)} %get-tuple-element.123, bf16[512,3,32]{0,2,1:T(8,128)(2,1)S(1)} %get-tuple-element.122, ...), kind=kOutput, calls=%fused_computation.130 | convolution fusion | flops 310636032 | bytes 10504192 | tf_op jit(solution)/shard_map/tkgd,skd->kgts/dot_general | solution.py:44
  60.3 2.3 copy-done.8
  62.6 1.7 fusion.16
  64.4 1.7 multiply_reduce_fusion.2
  71.2 2.9 %multiply_convert_fusion = (bf16[512,1536]{1,0:T(8,128)(2,1)S(1)}, bf16[512,1536]{1,0:T(8,128)(2,1)S(1)}, bf16[512,1536]{1,0:T(8,128)(2,1)S(1)}) fusion(f32[512,1536]{1,0:T(8,128)S(1)} %fusion.66, f32[512,1536]{1,0:T(8,128)S(1)} %fusion.67, bf16[1536,576]{1,0:T(8,128)(2,1)S(1)} %bitcast.239, bf16[1,512,576]{1,2,0:T(8,128)(2,1)S(1)} %copy-done.31), kind=kOutput, calls=%fused_computation.15 | convolution fusion | flops 918552576 | bytes 13369344 | tf_op jit(solution)/shard_map/td,fd->tf/dot_general | solution.py:384
  74.1 1.9 fusion.17
  78.6 1.7 multiply_subtract_fusion
  81.5 5.3 %fusion = (f32[3,3,512]{2,1,0:T(4,128)}, f32[3,512,512,3]{2,1,3,0:T(8,128)}) fusion(f32[3,3,512,512]{2,3,1,0:T(8,128)S(1)} %bitcast.209, f32[3,3,512]{2,1,0:T(4,128)S(1)} %log_add_fusion, bf16[512,3,64,1]{0,2,3,1:T(8,128)(2,1)S(1)} %bitcast.235, bf16[512,3,3,64]{0,3,2,1:T(8,128)(2,1)S(1)} %bitcast.216), kind=kOutput, calls=%fused_computation.2 | convolution fusion | flops 309063168 | bytes 19697664 | tf_op jit(solution)/shard_map/tkgd,skd->kgts/dot_general | solution.py:406
  86.8 11.1 %fusion.2 = bf16[3,3,512,512]{2,3,1,0:T(8,128)(2,1)} fusion(f32[3,512,512,3]{2,1,3,0:T(8,128)} %get-tuple-element.137, f32[3,3,512,512]{2,3,1,0:T(8,128)} %copy-done.8, f32[3,3,512]{2,1,0:T(4,128)} %get-tuple-element.136, f32[3,3,512]{2,1,0:T(4,128)} %copy-done.40), kind=kLoop, calls=%fused_computation.4 | loop fusion | flops 9437184 | bytes 23629824 | tf_op jit(solution)/shard_map/convert_element_type | solution.py:408
  98.0 3.5 %convolution_multiply_fusion = f32[3,64,3,512]{3,1,2,0:T(8,128)S(1)} fusion(bf16[3,3,512,512]{2,3,1,0:T(8,128)(2,1)} %fusion.2, bf16[512,3,32]{0,2,1:T(8,128)(2,1)} %copy-done.39, bf16[512,3,32]{0,2,1:T(8,128)(2,1)} %copy-done.38), kind=kOutput, calls=%fused_computation.32 | convolution fusion | flops 302678016 | bytes 6094848 | tf_op jit(solution)/shard_map/kgts,skd->tkgd/dot_general | solution.py:410
  101.5 1.8 multiply_subtract_fusion.1
  104.9 1.5 fusion.22
  107.7 1.6 fusion.34
  112.8 2.3 copy.41
  115.1 2.8 %convolution_convert_fusion.2 = bf16[576,1536]{1,0:T(8,128)(2,1)S(1)} fusion(bf16[512,576]{0,1:T(8,128)(2,1)} %copy-done.35, bf16[512,1536]{1,0:T(8,128)(2,1)} %copy-done.59), kind=kOutput, calls=%fused_computation.21 | convolution fusion | flops 906854400 | bytes 3932160 | tf_op jit(solution)/shard_map/td,tf->df/dot_general | solution.py:387
  118.0 2.3 %convolution_convert_fusion.1 = bf16[576,1536]{1,0:T(8,128)(2,1)} fusion(bf16[512,576]{0,1:T(8,128)(2,1)S(1)} %copy-done.36, bf16[512,1536]{1,0:T(8,128)(2,1)S(1)} %copy-done.56), kind=kOutput, calls=%fused_computation.20 | convolution fusion | flops 906854400 | bytes 3932160 | tf_op jit(solution)/shard_map/td,tf->df/dot_general | solution.py:388
  125.4 4.0 %concatenate.50.refs_3_ = bf16[2,288,1536]{2,1,0:T(8,128)(2,1)} concatenate(bf16[2,288,576]{2,1,0:T(8,128)(2,1)} %convolution_convert_fusion.4, bf16[2,288,192]{2,1,0:T(8,128)(2,1)S(1)} %copy-done.28, bf16[2,288,192]{2,1,0:T(8,128)(2,1)S(1)} %copy-done.29, bf16[2,288,576]{2,1,0:T(8,128)(2,1)} %convolution_convert_fusion.3), dimensions={2} | concatenate | bytes 3538944 | tf_op jit(solution)/shard_map/concatenate | solution.py:435
  131.0 85.2 %shard_map.204 = (bf16[1,768,576]{2,1,0:T(8,128)(2,1)S(1)}, bf16[1,288,1536]{2,1,0:T(8,128)(2,1)S(1)}, bf16[1,288,1536]{2,1,0:T(8,128)(2,1)S(1)}, bf16[1,288,1536]{2,1,0:T(8,128)(2,1)S(1)}, f32[1,8,576]{2,1,0:T(8,128)S(1)}) custom-call(bf16[2,768,576]{2,1,0:T(8,128)(2,1)} %bitcast.215, bf16[2,288,1536]{2,1,0:T(8,128)(2,1)S(1)} %bitcast.207, ...), custom_call_target="tpu_custom_call" | custom-call | tf_op jit(solution)/shard_map/pallas_call | solution.py:292
  223.3 2.3 bitcast_convert_fusion.1
  227.0 2.8 %copy.42 = f32[768,576]{0,1:T(8,128)} copy(f32[768,576]{1,0:T(8,128)} %bitcast_convert_fusion) | data formatting | bytes 3538944
  (195 shorter events, 43.3 us)
Async XLA Ops:
  0.7 3.0 %copy-start.50 = (bf16[288]{0:T(512)(128)(2,1)S(1)}, bf16[288]{0:T(512)(128)(2,1)}, u32[]{:S(2)}) copy-start(bf16[288]{0:T(512)(128)(2,1)} %param.23) | copy-start | bytes 1732
  0.7 3.1 %copy-start.51 = (bf16[288]{0:T(512)(128)(2,1)S(1)}, bf16[288]{0:T(512)(128)(2,1)}, u32[]{:S(2)}) copy-start(bf16[288]{0:T(512)(128)(2,1)} %param.28) | copy-start | bytes 1732
  7.3 36.1 %copy-start.14 = (bf16[1,512,576]{1,2,0:T(8,128)(2,1)S(1)}, bf16[1,512,576]{1,2,0:T(8,128)(2,1)}, u32[]{:S(2)}) copy-start(bf16[1,512,576]{1,2,0:T(8,128)(2,1)} %param.20) | copy-start | bytes 1769476
  46.7 7.9 %copy-start.12 = (bf16[1,512,576]{1,2,0:T(8,128)(2,1)}, bf16[1,512,576]{1,2,0:T(8,128)(2,1)S(1)}, u32[]{:S(2)}) copy-start(bf16[1,512,576]{1,2,0:T(8,128)(2,1)S(1)} %fusion.33) | copy-start | bytes 1769476
  46.7 3.0 %copy-start.48 = (s32[1,512]{1,0:T(1,128)S(1)}, s32[1,512]{1,0:T(1,128)}, u32[]{:S(2)}) copy-start(s32[1,512]{1,0:T(1,128)} %param.21) | copy-start | bytes 6148
  51.3 4.5 %copy-start.24 = (f32[512,32]{0,1:T(8,128)}, f32[512,32]{0,1:T(8,128)S(1)}, u32[]{:S(2)}) copy-start(f32[512,32]{0,1:T(8,128)S(1)} %get-tuple-element.126) | copy-start | bytes 196612
  55.9 2.9 %copy-start.38 = (bf16[512,3,32]{0,2,1:T(8,128)(2,1)}, bf16[512,3,32]{0,2,1:T(8,128)(2,1)S(1)}, u32[]{:S(2)}) copy-start(bf16[512,3,32]{0,2,1:T(8,128)(2,1)S(1)} %get-tuple-element.122) | copy-start | bytes 294916
  56.0 2.9 %copy-start.39 = (bf16[512,3,32]{0,2,1:T(8,128)(2,1)}, bf16[512,3,32]{0,2,1:T(8,128)(2,1)S(1)}, u32[]{:S(2)}) copy-start(bf16[512,3,32]{0,2,1:T(8,128)(2,1)S(1)} %get-tuple-element.123) | copy-start | bytes 294916
  58.9 3.7 %copy-start.8 = (f32[3,3,512,512]{2,3,1,0:T(8,128)}, f32[3,3,512,512]{2,3,1,0:T(8,128)S(1)}, u32[]{:S(2)}) copy-start(f32[3,3,512,512]{2,3,1,0:T(8,128)S(1)} %get-tuple-element.132) | copy-start | bytes 28311556
  58.9 3.7 %copy-start.44 = (f32[3,3,512]{2,1,0:T(4,128)}, f32[3,3,512]{2,1,0:T(4,128)S(1)}, u32[]{:S(2)}) copy-start(f32[3,3,512]{2,1,0:T(4,128)S(1)} %get-tuple-element.131) | copy-start | bytes 55300
  58.9 3.7 %copy-start.42 = (bf16[512,192]{0,1:T(8,128)(2,1)S(1)}, bf16[512,192]{0,1:T(8,128)(2,1)}, u32[]{:S(2)}) copy-start(bf16[512,192]{0,1:T(8,128)(2,1)} %convolution_convert_fusion.8) | copy-start | bytes 589828
  66.0 11.1 %copy-start.17 = (f32[512,576]{0,1:T(8,128)}, f32[512,576]{0,1:T(8,128)S(1)}, u32[]{:S(2)}) copy-start(f32[512,576]{0,1:T(8,128)S(1)} %get-tuple-element.134) | copy-start | bytes 3538948
  74.1 3.1 %copy-start.55 = (bf16[512,1536]{1,0:T(8,128)(2,1)}, bf16[512,1536]{1,0:T(8,128)(2,1)S(1)}, u32[]{:S(2)}) copy-start(bf16[512,1536]{1,0:T(8,128)(2,1)S(1)} %get-tuple-element.109) | copy-start | bytes 4718596
  74.1 7.0 %slice-start = ((s8[9437184]{0:T(1024)(128)(4,1)}), s8[4194304]{0:T(1024)(128)(4,1)S(1)}, s32[]{:S(2)}) async-start(s8[9437184]{0:T(1024)(128)(4,1)} %bitcast.208), calls=%async_computation | async-start | bytes 8388608
  76.0 5.1 %slice-start.1 = ((s8[9437184]{0:T(1024)(128)(4,1)}), s8[4194304]{0:T(1024)(128)(4,1)S(1)}, s32[]{:S(2)}) async-start(s8[9437184]{0:T(1024)(128)(4,1)} %bitcast.208), calls=%async_computation.1 | async-start | bytes 8388608
  77.2 4.0 %slice-start.2 = ((s8[9437184]{0:T(1024)(128)(4,1)}), s8[1048576]{0:T(1024)(128)(4,1)S(1)}, s32[]{:S(2)}) async-start(s8[9437184]{0:T(1024)(128)(4,1)} %bitcast.208), calls=%async_computation.2 | async-start | bytes 2097152
  80.4 29.6 %copy-start.10 = (f32[512,576]{0,1:T(8,128)}, f32[512,576]{0,1:T(8,128)S(1)}, u32[]{:S(2)}) copy-start(f32[512,576]{0,1:T(8,128)S(1)} %multiply_subtract_fusion) | copy-start | bytes 3538948
  80.4 6.4 %copy-start.40 = (f32[3,3,512]{2,1,0:T(4,128)}, f32[3,3,512]{2,1,0:T(4,128)S(1)}, u32[]{:S(2)}) copy-start(f32[3,3,512]{2,1,0:T(4,128)S(1)} %log_add_fusion) | copy-start | bytes 55300
  81.1 5.7 %copy-start.15 = (bf16[512,576]{0,1:T(8,128)(2,1)}, bf16[512,576]{0,1:T(8,128)(2,1)S(1)}, u32[]{:S(2)}) copy-start(bf16[512,576]{0,1:T(8,128)(2,1)S(1)} %convolution_convert_fusion.5) | copy-start | bytes 1769476
  98.0 6.9 %copy-start.9 = (bf16[3,3,512,512]{2,3,1,0:T(8,128)(2,1)S(1)}, bf16[3,3,512,512]{2,3,1,0:T(8,128)(2,1)}, u32[]{:S(2)}) copy-start(bf16[3,3,512,512]{2,3,1,0:T(8,128)(2,1)} %fusion.2) | copy-start | bytes 14155780
  98.0 6.9 %copy-start.26 = (bf16[512,9,32]{0,2,1:T(8,128)(2,1)S(1)}, bf16[512,9,32]{0,2,1:T(8,128)(2,1)}, u32[]{:S(2)}) copy-start(bf16[512,9,32]{0,2,1:T(8,128)(2,1)} %get-tuple-element.118) | copy-start | bytes 884740
  98.0 6.9 %copy-start.27 = (bf16[512,9,32]{0,2,1:T(8,128)(2,1)S(1)}, bf16[512,9,32]{0,2,1:T(8,128)(2,1)}, u32[]{:S(2)}) copy-start(bf16[512,9,32]{0,2,1:T(8,128)(2,1)} %get-tuple-element.119) | copy-start | bytes 884740
  98.0 9.7 %slice-start.3 = ((s8[9437184]{0:T(1024)(128)(4,1)}), s8[4194304]{0:T(1024)(128)(4,1)S(1)}, s32[]{:S(2)}) async-start(s8[9437184]{0:T(1024)(128)(4,1)} %bitcast.210), calls=%async_computation.3 | async-start | bytes 8388608
  101.5 6.2 %slice-start.4 = ((s8[9437184]{0:T(1024)(128)(4,1)}), s8[4194304]{0:T(1024)(128)(4,1)S(1)}, s32[]{:S(2)}) async-start(s8[9437184]{0:T(1024)(128)(4,1)} %bitcast.210), calls=%async_computation.4 | async-start | bytes 8388608
  (42 other events, 69.8 us)

commit v2 on v1

--- a/solution.py
+++ b/solution.py
@@ -159,7 +159,9 @@
     rep_bits, shard_bits = bits_of(reps), list(reversed(bits_of(shards)))
     size = list(shape)
     order = [("rep", b) for b in rep_bits]
-    first = 2 if turn % 2 else 1
+    if turn in "ZWU" and len(order) > 3:
+        order[1], order[2] = order[2], order[1]
+    first = {"Y": 1, "W": 1, "X": 2, "Z": 2, "V": 3, "U": 3}[turn]
     order[first:first] = [("shard", b) for b in shard_bits]
     steps = []
     for n, (axis, bit) in enumerate(order):
@@ -177,9 +179,19 @@
     return steps
 
 
-def reduce_kernel(plans, shards, count, *refs):
-    grads, outs = refs[:count], refs[count : 2 * count]
-    refs = refs[2 * count :]
+def piece_of(ref, dim, base, size):
+    if dim is None:
+        return ref
+    cut = [slice(None)] * 3
+    cut[dim] = pl.ds(base, size)
+    return ref.at[tuple(cut)]
+
+
+def reduce_kernel(plans, pieces, arrays, *refs):
+    count = len(pieces)
+    grads = [piece_of(refs[a], *cut) for a, *cut in pieces]
+    outs = [piece_of(refs[arrays + a], *cut) for a, *cut in pieces]
+    refs = refs[2 * arrays :]
     send, recv = refs[-2:]
     lands, at = [], 0
     for plan in plans:
@@ -216,7 +228,7 @@
         link = (axis, bit)
         rate = 300e3 if link == ("rep", 1) else 50e3
         begin = max(clock[0], free.get(link, 0.0))
-        free[link] = begin + math.prod(src.shape) * 2 / rate
+        free[link] = begin + math.prod(dst.shape) * 2 / rate
         return go, free[link] + 1.5
 
     def stream(c):
@@ -281,23 +293,34 @@
         go.wait_send()
 
 
-def reduce_grads(grads, splits, shards, reps):
-    plans = [plan_of(g.shape, shards, reps, cut, i) for i, (g, cut) in enumerate(zip(grads, splits))]
-    outs, lands, most = [], [], 0
-    for g, plan, cut in zip(grads, plans, splits):
-        lead = 1 if cut else g.shape[0]
-        outs.append(jax.ShapeDtypeStruct((lead,) + g.shape[1:], g.dtype))
-        lands += [pltpu.VMEM(after, g.dtype) for _, _, _, after in plan]
-        most = max(most, 2 * len(plan))
+TURNS = "WUUYYYYYVZZY"
+
+
+def reduce_grads(grads, cuts, shards, reps):
+    plans, pieces, lands, outs = [], [], [], []
+    for a, (g, dim) in enumerate(zip(grads, cuts)):
+        outs.append(jax.ShapeDtypeStruct((1 if dim else g.shape[0],) + g.shape[1:], g.dtype))
+        number = 3 if dim else 1
+        for n in range(number):
+            shape = list(g.shape)
+            if dim:
+                shape[dim] //= number
+            turn = TURNS[len(pieces) % len(TURNS)]
+            plan = plan_of(tuple(shape), shards, reps, dim is not None, turn)
+            size = shape[dim] if dim else 0
+            pieces.append((a, dim, n * size, size))
+            plans.append(plan)
+            lands += [pltpu.VMEM(after, g.dtype) for _, _, _, after in plan]
+    most = max(2 * len(plan) for plan in plans)
     return pl.pallas_call(
-        functools.partial(reduce_kernel, plans, shards, len(grads)),
+        functools.partial(reduce_kernel, plans, pieces, len(grads)),
         out_shape=outs,
         in_specs=[pl.BlockSpec(memory_space=pltpu.VMEM)] * len(grads),
         out_specs=[pl.BlockSpec(memory_space=pltpu.VMEM)] * len(grads),
         scratch_shapes=lands
         + [
-            pltpu.SemaphoreType.DMA((len(grads), most)),
-            pltpu.SemaphoreType.DMA((len(grads), most)),
+            pltpu.SemaphoreType.DMA((len(pieces), most)),
+            pltpu.SemaphoreType.DMA((len(pieces), most)),
         ],
         compiler_params=pltpu.CompilerParams(
             collective_id=1, has_side_effects=True, vmem_limit_bytes=VMEM_LIMIT
@@ -439,7 +462,7 @@
         g.astype(low).reshape(shards, -1, g.shape[1])
         for g in (grad_down, grad_gate, grad_up, g_attn)
     ]
-    sums = reduce_grads(parts + [g_gains], [True] * 4 + [False], shards, reps)
+    sums = reduce_grads(parts + [g_gains], [1, 2, 2, 2, None], shards, reps)
     t_down, t_gate, t_up, t_attn = [t[0].astype(jnp.float32) for t in sums[:4]]
     g_gains = sums[4][0, :2]
     own = width // shards

time: 231 us -> 213 us (0.922)
  Pallas kernels: 121 us -> 103 us
    pallas_call x1, Pallas kernels: 85.2 us -> 67.4 us  [reduce_grads(): pl.pallas_call(functools.partial(reduce_kernel, plans, pieces, len(grads)...]
where the time goes in v2:
time: 213 us; the launch traced here: 212 us
  Pallas kernels  103 us (48%)
  matrix products  47.1 us (22%)
  local copies, waits for them, and re-layouts  31.7 us (15%)
  other arithmetic  28.3 us (13%)
    pallas_call x1, Pallas kernels, reduce_grads(): pl.pallas_call(functools.partial(reduce_kernel, plans, pieces, len(grads)...  67.4 us
    pallas_call x1, Pallas kernels, gather_weights(): pl.pallas_call(functools.partial(gather_kernel, shards, share, dims), out...  35.9 us
    unnamed x134, local copies, waits for them, and re-layouts  15.9 us
    convert_element_type x1, other arithmetic, body(): d_scores = (probs_f * (d_probs - delta)).astype(jnp.bfloat16)  11.1 us
    dot_general x1, matrix products, body(): jnp.einsum('tkgd,skd->kgts', d_mixed, values, preferred_element_type=jnp....  5.32 us
    convert_element_type x3, other arithmetic, body(): t_down, t_gate, t_up, t_attn = [t[0].astype(jnp.float32) for t in sums[:4]]  5.06 us

profile of v2, /device:TPU:0, one launch (start us, length us, event | category | flops | bytes accessed | tf_op | source)
XLA Modules:
  0.0 211.9 jit_solution(14774913403584996192)
XLA Ops:
  0.7 2.4 %concatenate.41.refs_0_ = bf16[288,1536]{1,0:T(8,128)(2,1)} concatenate(bf16[288,576]{1,0:T(8,128)(2,1)} %param.24, bf16[288,192]{1,0:T(8,128)(2,1)} %param.25, bf16[288,192]{1,0:T(8,128)(2,1)} %param.26, bf16[288,576]{1,0:T(8,128)(2,1)} %param.27), dimensions={1} | concatenate | bytes 1769472 | tf_op jit(solution)/shard_map/concatenate | solution.py:348
  7.3 35.9 %shard_map.203 = (bf16[2,288,1536]{2,1,0:T(8,128)(2,1)S(1)}, bf16[2,288,1536]{2,1,0:T(8,128)(2,1)}, bf16[2,288,1536]{2,1,0:T(8,128)(2,1)}, bf16[2,768,576]{2,1,0:T(8,128)(2,1)}, bf16[2,16,288]{2,1,0:T(8,128)(2,1)S(1)}) custom-call(bf16[288,1536]{1,0:T(8,128)(2,1)S(1)} %copy-done, bf16[288,1536]{1,0:T(8,128)(2,1)S(1)} %copy-done.1, ...), custom_call_target="tpu_custom_call" | custom-call | tf_op jit(solution)/shard_map/pallas_call | solution.py:142
  46.7 3.0 %fusion.47 = f32[512,9,64]{0,2,1:T(8,128)} fusion(bf16[9,64,576]{2,1,0:T(8,128)(2,1)} %bitcast.231, bf16[1,512,576]{1,2,0:T(8,128)(2,1)S(1)} %fusion.33), kind=kOutput, calls=%fused_computation.82 | convolution fusion | flops 339738624 | bytes 2433024 | tf_op jit(solution)/shard_map/dot_general | solution.py:373
  51.3 2.3 %subtract_convert_fusion = (bf16[512,9,32]{0,2,1:T(8,128)(2,1)}, bf16[512,9,32]{0,2,1:T(8,128)(2,1)}) fusion(f32[512,9,64]{0,2,1:T(8,128)} %fusion.47, f32[512,32]{0,1:T(8,128)S(1)} %get-tuple-element.125, f32[512,32]{0,1:T(8,128)S(1)} %get-tuple-element.126), kind=kLoop, calls=%fused_computation.89 | loop fusion | flops 1179648 | bytes 1900544 | tf_op jit(solution)/shard_map/convert.14
  56.2 2.7 %fusion.65 = (f32[3,3,512]{2,1,0:T(4,128)S(1)}, f32[3,3,512,512]{2,3,1,0:T(8,128)S(1)}) fusion(bf16[512,3,3,32]{0,3,2,1:T(8,128)(2,1)} %bitcast.228, bf16[512,3,3,32]{0,3,2,1:T(8,128)(2,1)} %bitcast.226, bf16[512,3,32]{0,2,1:T(8,128)(2,1)S(1)} %get-tuple-element.123, bf16[512,3,32]{0,2,1:T(8,128)(2,1)S(1)} %get-tuple-element.122, ...), kind=kOutput, calls=%fused_computation.130 | convolution fusion | flops 310636032 | bytes 10504192 | tf_op jit(solution)/shard_map/tkgd,skd->kgts/dot_general | solution.py:44
  60.3 2.3 %copy-done.8 = f32[3,3,512,512]{2,3,1,0:T(8,128)} copy-done((f32[3,3,512,512]{2,3,1,0:T(8,128)}, f32[3,3,512,512]{2,3,1,0:T(8,128)S(1)}, u32[]{:S(2)}) %copy-start.8) | copy-done | bytes 9437208
  62.6 1.7 fusion.16
  64.4 1.7 multiply_reduce_fusion.2
  71.2 2.9 %multiply_convert_fusion = (bf16[512,1536]{1,0:T(8,128)(2,1)S(1)}, bf16[512,1536]{1,0:T(8,128)(2,1)S(1)}, bf16[512,1536]{1,0:T(8,128)(2,1)S(1)}) fusion(f32[512,1536]{1,0:T(8,128)S(1)} %fusion.66, f32[512,1536]{1,0:T(8,128)S(1)} %fusion.67, bf16[1536,576]{1,0:T(8,128)(2,1)S(1)} %bitcast.239, bf16[1,512,576]{1,2,0:T(8,128)(2,1)S(1)} %copy-done.31), kind=kOutput, calls=%fused_computation.15 | convolution fusion | flops 918552576 | bytes 13369344 | tf_op jit(solution)/shard_map/td,fd->tf/dot_general | solution.py:407
  74.1 1.9 fusion.17
  78.6 1.7 multiply_subtract_fusion
  81.5 5.3 %fusion = (f32[3,3,512]{2,1,0:T(4,128)}, f32[3,512,512,3]{2,1,3,0:T(8,128)}) fusion(f32[3,3,512,512]{2,3,1,0:T(8,128)S(1)} %bitcast.209, f32[3,3,512]{2,1,0:T(4,128)S(1)} %log_add_fusion, bf16[512,3,64,1]{0,2,3,1:T(8,128)(2,1)S(1)} %bitcast.235, bf16[512,3,3,64]{0,3,2,1:T(8,128)(2,1)S(1)} %bitcast.216), kind=kOutput, calls=%fused_computation.2 | convolution fusion | flops 309063168 | bytes 19697664 | tf_op jit(solution)/shard_map/tkgd,skd->kgts/dot_general | solution.py:429
  86.8 11.1 %fusion.2 = bf16[3,3,512,512]{2,3,1,0:T(8,128)(2,1)} fusion(f32[3,512,512,3]{2,1,3,0:T(8,128)} %get-tuple-element.137, f32[3,3,512,512]{2,3,1,0:T(8,128)} %copy-done.8, f32[3,3,512]{2,1,0:T(4,128)} %get-tuple-element.136, f32[3,3,512]{2,1,0:T(4,128)} %copy-done.40), kind=kLoop, calls=%fused_computation.4 | loop fusion | flops 9437184 | bytes 23629824 | tf_op jit(solution)/shard_map/convert_element_type | solution.py:431
  98.0 3.5 %convolution_multiply_fusion = f32[3,64,3,512]{3,1,2,0:T(8,128)S(1)} fusion(bf16[3,3,512,512]{2,3,1,0:T(8,128)(2,1)} %fusion.2, bf16[512,3,32]{0,2,1:T(8,128)(2,1)} %copy-done.39, bf16[512,3,32]{0,2,1:T(8,128)(2,1)} %copy-done.38), kind=kOutput, calls=%fused_computation.32 | convolution fusion | flops 302678016 | bytes 6094848 | tf_op jit(solution)/shard_map/kgts,skd->tkgd/dot_general | solution.py:433
  101.5 1.8 multiply_subtract_fusion.1
  104.9 1.5 fusion.22
  107.7 1.6 fusion.34
  112.8 2.3 %copy.41 = bf16[1536,576]{1,0:T(8,128)(2,1)} copy(bf16[1536,576]{0,1:T(8,128)(2,1)S(1)} %convolution_convert_fusion) | data formatting | bytes 3538944 | tf_op jit(solution)/shard_map/convert_element_type | solution.py:462
  115.1 2.8 %convolution_convert_fusion.2 = bf16[576,1536]{1,0:T(8,128)(2,1)S(1)} fusion(bf16[512,576]{0,1:T(8,128)(2,1)} %copy-done.35, bf16[512,1536]{1,0:T(8,128)(2,1)} %copy-done.59), kind=kOutput, calls=%fused_computation.21 | convolution fusion | flops 906854400 | bytes 3932160 | tf_op jit(solution)/shard_map/td,tf->df/dot_general | solution.py:410
  118.0 2.3 %convolution_convert_fusion.1 = bf16[576,1536]{1,0:T(8,128)(2,1)} fusion(bf16[512,576]{0,1:T(8,128)(2,1)S(1)} %copy-done.36, bf16[512,1536]{1,0:T(8,128)(2,1)S(1)} %copy-done.56), kind=kOutput, calls=%fused_computation.20 | convolution fusion | flops 906854400 | bytes 3932160 | tf_op jit(solution)/shard_map/td,tf->df/dot_general | solution.py:411
  125.4 4.0 %concatenate.50.refs_3_ = bf16[2,288,1536]{2,1,0:T(8,128)(2,1)} concatenate(bf16[2,288,576]{2,1,0:T(8,128)(2,1)} %convolution_convert_fusion.4, bf16[2,288,192]{2,1,0:T(8,128)(2,1)S(1)} %copy-done.28, bf16[2,288,192]{2,1,0:T(8,128)(2,1)S(1)} %copy-done.29, bf16[2,288,576]{2,1,0:T(8,128)(2,1)} %convolution_convert_fusion.3), dimensions={2} | concatenate | bytes 3538944 | tf_op jit(solution)/shard_map/concatenate | solution.py:458
  131.0 67.4 %shard_map.204 = (bf16[1,768,576]{2,1,0:T(8,128)(2,1)S(1)}, bf16[1,288,1536]{2,1,0:T(8,128)(2,1)S(1)}, bf16[1,288,1536]{2,1,0:T(8,128)(2,1)S(1)}, bf16[1,288,1536]{2,1,0:T(8,128)(2,1)S(1)}, f32[1,8,576]{2,1,0:T(8,128)S(1)}) custom-call(bf16[2,768,576]{2,1,0:T(8,128)(2,1)} %bitcast.215, bf16[2,288,1536]{2,1,0:T(8,128)(2,1)S(1)} %bitcast.207, ...), custom_call_target="tpu_custom_call" | custom-call | tf_op jit(solution)/shard_map/pallas_call | solution.py:315
  205.5 2.3 %bitcast_convert_fusion.1 = (f32[288,1536]{1,0:T(8,128)}, f32[288,1536]{1,0:T(8,128)}) fusion(bf16[1,288,1536]{2,1,0:T(8,128)(2,1)S(1)} %copy-done.7, bf16[1,288,1536]{2,1,0:T(8,128)(2,1)S(1)} %copy-done.5), kind=kLoop, calls=%fused_computation.69 | loop fusion | flops 884736 | bytes 5308416 | tf_op jit(solution)/shard_map/convert_element_type | solution.py:466
  209.2 2.8 %copy.42 = f32[768,576]{0,1:T(8,128)} copy(f32[768,576]{1,0:T(8,128)} %bitcast_convert_fusion) | data formatting | bytes 3538944
  (195 shorter events, 43.3 us)
Async XLA Ops:
  0.7 3.0 %copy-start.50 = (bf16[288]{0:T(512)(128)(2,1)S(1)}, bf16[288]{0:T(512)(128)(2,1)}, u32[]{:S(2)}) copy-start(bf16[288]{0:T(512)(128)(2,1)} %param.23) | copy-start | bytes 1732
  0.7 3.1 %copy-start.51 = (bf16[288]{0:T(512)(128)(2,1)S(1)}, bf16[288]{0:T(512)(128)(2,1)}, u32[]{:S(2)}) copy-start(bf16[288]{0:T(512)(128)(2,1)} %param.28) | copy-start | bytes 1732
  7.3 36.1 %copy-start.14 = (bf16[1,512,576]{1,2,0:T(8,128)(2,1)S(1)}, bf16[1,512,576]{1,2,0:T(8,128)(2,1)}, u32[]{:S(2)}) copy-start(bf16[1,512,576]{1,2,0:T(8,128)(2,1)} %param.20) | copy-start | bytes 1769476
  46.7 7.9 %copy-start.12 = (bf16[1,512,576]{1,2,0:T(8,128)(2,1)}, bf16[1,512,576]{1,2,0:T(8,128)(2,1)S(1)}, u32[]{:S(2)}) copy-start(bf16[1,512,576]{1,2,0:T(8,128)(2,1)S(1)} %fusion.33) | copy-start | bytes 1769476
  46.7 3.0 %copy-start.48 = (s32[1,512]{1,0:T(1,128)S(1)}, s32[1,512]{1,0:T(1,128)}, u32[]{:S(2)}) copy-start(s32[1,512]{1,0:T(1,128)} %param.21) | copy-start | bytes 6148
  51.3 4.5 %copy-start.24 = (f32[512,32]{0,1:T(8,128)}, f32[512,32]{0,1:T(8,128)S(1)}, u32[]{:S(2)}) copy-start(f32[512,32]{0,1:T(8,128)S(1)} %get-tuple-element.126) | copy-start | bytes 196612
  55.9 2.9 %copy-start.38 = (bf16[512,3,32]{0,2,1:T(8,128)(2,1)}, bf16[512,3,32]{0,2,1:T(8,128)(2,1)S(1)}, u32[]{:S(2)}) copy-start(bf16[512,3,32]{0,2,1:T(8,128)(2,1)S(1)} %get-tuple-element.122) | copy-start | bytes 294916
  56.0 2.9 %copy-start.39 = (bf16[512,3,32]{0,2,1:T(8,128)(2,1)}, bf16[512,3,32]{0,2,1:T(8,128)(2,1)S(1)}, u32[]{:S(2)}) copy-start(bf16[512,3,32]{0,2,1:T(8,128)(2,1)S(1)} %get-tuple-element.123) | copy-start | bytes 294916
  58.9 3.7 %copy-start.8 = (f32[3,3,512,512]{2,3,1,0:T(8,128)}, f32[3,3,512,512]{2,3,1,0:T(8,128)S(1)}, u32[]{:S(2)}) copy-start(f32[3,3,512,512]{2,3,1,0:T(8,128)S(1)} %get-tuple-element.132) | copy-start | bytes 28311556
  58.9 3.7 %copy-start.44 = (f32[3,3,512]{2,1,0:T(4,128)}, f32[3,3,512]{2,1,0:T(4,128)S(1)}, u32[]{:S(2)}) copy-start(f32[3,3,512]{2,1,0:T(4,128)S(1)} %get-tuple-element.131) | copy-start | bytes 55300
  58.9 3.7 %copy-start.42 = (bf16[512,192]{0,1:T(8,128)(2,1)S(1)}, bf16[512,192]{0,1:T(8,128)(2,1)}, u32[]{:S(2)}) copy-start(bf16[512,192]{0,1:T(8,128)(2,1)} %convolution_convert_fusion.8) | copy-start | bytes 589828
  66.0 11.1 %copy-start.17 = (f32[512,576]{0,1:T(8,128)}, f32[512,576]{0,1:T(8,128)S(1)}, u32[]{:S(2)}) copy-start(f32[512,576]{0,1:T(8,128)S(1)} %get-tuple-element.134) | copy-start | bytes 3538948
  74.1 3.1 %copy-start.55 = (bf16[512,1536]{1,0:T(8,128)(2,1)}, bf16[512,1536]{1,0:T(8,128)(2,1)S(1)}, u32[]{:S(2)}) copy-start(bf16[512,1536]{1,0:T(8,128)(2,1)S(1)} %get-tuple-element.109) | copy-start | bytes 4718596
  74.1 7.0 %slice-start = ((s8[9437184]{0:T(1024)(128)(4,1)}), s8[4194304]{0:T(1024)(128)(4,1)S(1)}, s32[]{:S(2)}) async-start(s8[9437184]{0:T(1024)(128)(4,1)} %bitcast.208), calls=%async_computation | async-start | bytes 8388608
  76.0 5.1 %slice-start.1 = ((s8[9437184]{0:T(1024)(128)(4,1)}), s8[4194304]{0:T(1024)(128)(4,1)S(1)}, s32[]{:S(2)}) async-start(s8[9437184]{0:T(1024)(128)(4,1)} %bitcast.208), calls=%async_computation.1 | async-start | bytes 8388608
  77.2 4.0 %slice-start.2 = ((s8[9437184]{0:T(1024)(128)(4,1)}), s8[1048576]{0:T(1024)(128)(4,1)S(1)}, s32[]{:S(2)}) async-start(s8[9437184]{0:T(1024)(128)(4,1)} %bitcast.208), calls=%async_computation.2 | async-start | bytes 2097152
  80.4 29.6 %copy-start.10 = (f32[512,576]{0,1:T(8,128)}, f32[512,576]{0,1:T(8,128)S(1)}, u32[]{:S(2)}) copy-start(f32[512,576]{0,1:T(8,128)S(1)} %multiply_subtract_fusion) | copy-start | bytes 3538948
  80.4 6.4 %copy-start.40 = (f32[3,3,512]{2,1,0:T(4,128)}, f32[3,3,512]{2,1,0:T(4,128)S(1)}, u32[]{:S(2)}) copy-start(f32[3,3,512]{2,1,0:T(4,128)S(1)} %log_add_fusion) | copy-start | bytes 55300
  81.1 5.7 %copy-start.15 = (bf16[512,576]{0,1:T(8,128)(2,1)}, bf16[512,576]{0,1:T(8,128)(2,1)S(1)}, u32[]{:S(2)}) copy-start(bf16[512,576]{0,1:T(8,128)(2,1)S(1)} %convolution_convert_fusion.5) | copy-start | bytes 1769476
  98.0 6.9 %copy-start.9 = (bf16[3,3,512,512]{2,3,1,0:T(8,128)(2,1)S(1)}, bf16[3,3,512,512]{2,3,1,0:T(8,128)(2,1)}, u32[]{:S(2)}) copy-start(bf16[3,3,512,512]{2,3,1,0:T(8,128)(2,1)} %fusion.2) | copy-start | bytes 14155780
  98.0 6.9 %copy-start.26 = (bf16[512,9,32]{0,2,1:T(8,128)(2,1)S(1)}, bf16[512,9,32]{0,2,1:T(8,128)(2,1)}, u32[]{:S(2)}) copy-start(bf16[512,9,32]{0,2,1:T(8,128)(2,1)} %get-tuple-element.118) | copy-start | bytes 884740
  98.0 6.9 %copy-start.27 = (bf16[512,9,32]{0,2,1:T(8,128)(2,1)S(1)}, bf16[512,9,32]{0,2,1:T(8,128)(2,1)}, u32[]{:S(2)}) copy-start(bf16[512,9,32]{0,2,1:T(8,128)(2,1)} %get-tuple-element.119) | copy-start | bytes 884740
  98.0 9.7 %slice-start.3 = ((s8[9437184]{0:T(1024)(128)(4,1)}), s8[4194304]{0:T(1024)(128)(4,1)S(1)}, s32[]{:S(2)}) async-start(s8[9437184]{0:T(1024)(128)(4,1)} %bitcast.210), calls=%async_computation.3 | async-start | bytes 8388608
  101.5 6.2 %slice-start.4 = ((s8[9437184]{0:T(1024)(128)(4,1)}), s8[4194304]{0:T(1024)(128)(4,1)S(1)}, s32[]{:S(2)}) async-start(s8[9437184]{0:T(1024)(128)(4,1)} %bitcast.210), calls=%async_computation.4 | async-start | bytes 8388608
  (42 other events, 69.8 us)
